TPU v7x, 32 devices: a whole 2x2x4 slice. The times are simulated.
32 devices in a mesh: groups: 2 (over x), dp: 16 (over z, y, core).
Axes of the slice: x: 2, y: 2, z: 4, core: 2. Of those that a mesh axis runs over, the one named last changes fastest.
Arguments:
- queries: bfloat16 [24576, 4096], P(('groups', 'dp')), parts along dimension 0, may hold values from -120 to 120
- keys: bfloat16 [24576, 512], P(('groups', 'dp')), parts along dimension 0, may hold values from -6 to 6
- values: bfloat16 [24576, 512], P(('groups', 'dp')), parts along dimension 0, may hold values from -6 to 6
- block_counts: int32 [32], P(('groups', 'dp')), parts along dimension 0, may hold values from 0 to 6, as said below
- segment_ids: int32 [8192], P(('groups', 'dp')), parts along dimension 0, may hold values from 0 to 7, never falling along the last dimension, each value on 1 to 1024 neighbouring positions
- reward_dir: float32 [4096], replicated, may hold values from -4 to 4
Outputs:
- attn_out: bfloat16 [8192, 4096], P(('groups', 'dp')), parts along dimension 0
- rewards: float32 [16], P('groups'), parts along dimension 0
There are 2 independent parts, one for each index of `groups`. A program takes and returns all parts, laid end to end along the dimension named above; an argument that names none is the same for every part. Nothing has to cross between parts.
Inputs may be any that keep to these rules, and one draw needn't show every extreme that they name: `block_counts`: the counts sum to 2 times the number of ranks; for each rank s the counts of the ranks before s sum to between (2 * s - 2) and (2 * s + 2); some rank holds 6. `segment_ids`: positions never fall in segment number, each of the 8 responses holds 1 to 1024 positions.
All inputs are finite; a program needn't handle non-finite values.
Results may differ from a plain program's by a relative error of at most 0.0039.
The roundings to bfloat16 on the way count: a program that leaves them out, or rounds other values in their place, can miss the bound.
Values may be sent and summed in bfloat16 or wider, within the bound.
A program may use at most 128 MiB of HBM per device.

v0:
```python
import jax
import jax.numpy as jnp
from jax import lax
from jax.sharding import PartitionSpec as P

D_HEAD = 128
HEADS = 32
KV_HEADS = 4
BLOCK = 128
RECV = 2
REACH = 4


def prefix_2(part, axis, combine, identity):
    place = lax.axis_index(axis)
    gathered = jax.tree.map(lambda a: lax.all_gather(a, axis), part)
    state = jax.tree.map(lambda a, e: jnp.zeros_like(a) + jnp.asarray(e, a.dtype), part, identity)

    def one(hop, state):
        return combine(
            state, jax.tree.map(lambda a: lax.dynamic_index_in_dim(a, hop, 0, False), gathered)
        )

    return lax.fori_loop(0, place, one, state)


def shifted(block, axis, distance):
    devices = range(lax.axis_size(axis))
    route = [(i - distance, i) for i in devices if i - distance in devices]
    return lax.ppermute(block, axis, route)


def shortened(shard):
    return jax.tree.map(lambda a: a.astype(jnp.bfloat16) if a.dtype == jnp.float32 else a, shard)


def attend(query_rows, key_window, value_window, allowed):
    per_group = HEADS // KV_HEADS
    row_count = query_rows.shape[0]
    score_scale = D_HEAD ** (-0.5)
    grouped = query_rows.reshape(row_count, KV_HEADS, per_group, D_HEAD)
    key_heads = key_window.reshape(-1, KV_HEADS, D_HEAD)
    value_heads = value_window.reshape(-1, KV_HEADS, D_HEAD)
    head_outs = []
    for head_index in range(KV_HEADS):
        query_head = grouped[:, head_index].reshape(row_count * per_group, D_HEAD)
        logits = (
            jnp.dot(query_head, key_heads[:, head_index].T, preferred_element_type=jnp.float32)
            * score_scale
        )
        logits = logits.reshape(row_count, per_group, -1)
        logits = jnp.where(allowed[:, None, :], logits, -1e30)
        row_max = jnp.max(logits, axis=-1, keepdims=True)
        raised = jnp.exp(logits - row_max)
        totals = jnp.sum(raised, axis=-1)
        soft_weights = raised.astype(jnp.bfloat16).reshape(row_count * per_group, -1)
        head_out = jnp.dot(
            soft_weights, value_heads[:, head_index], preferred_element_type=jnp.float32
        )
        head_out = head_out.reshape(row_count, per_group, D_HEAD) / totals[..., None]
        head_outs.append(head_out.astype(jnp.bfloat16))
    return jnp.stack(head_outs, axis=1).reshape(row_count, HEADS * D_HEAD)


def combine_all(earlier, later):
    count_a, first_a, last_a, start_a = earlier
    count_b, first_b, last_b, start_b = later
    joined = (first_b == last_b) & (last_a == first_b)
    empty_b = last_b < 0
    return (
        count_a + count_b,
        jnp.where(first_a < 0, first_b, first_a),
        jnp.where(empty_b, last_a, last_b),
        jnp.where(empty_b | joined, start_a, start_b),
    )


def shards(queries, keys, values, block_counts, segment_ids, reward_dir):
    row_count = segment_ids.shape[0]
    capacity = queries.shape[0] // BLOCK
    own_rank = lax.axis_index("dp")
    own_count = block_counts[0]
    positions = jnp.arange(row_count, dtype=jnp.int32)
    base_row = own_rank * row_count
    changed = jnp.concatenate([jnp.ones((1,), bool), segment_ids[1:] != segment_ids[:-1]])
    local_start = lax.cummax(jnp.where(changed, positions, 0), axis=0)
    summary = (
        block_counts,
        segment_ids[0:1],
        segment_ids[row_count - 1 : row_count],
        base_row + local_start[row_count - 1 : row_count],
    )
    neutral = (
        jnp.zeros((1,), jnp.int32),
        jnp.full((1,), -1, jnp.int32),
        jnp.full((1,), -1, jnp.int32),
        jnp.zeros((1,), jnp.int32),
    )
    prefix = prefix_2(summary, "dp", combine_all, neutral)
    offset = prefix[0][0]
    starts = jnp.where(segment_ids == prefix[2][0], prefix[3][0], base_row + local_start)
    following = shifted(segment_ids[0:1] + 1, "dp", -1)[0] - 1
    next_ids = jnp.concatenate([segment_ids[1:], following[None]])
    is_last = segment_ids != next_ids

    def outgoing(members, distance):
        first_pick = (own_rank + distance) * RECV - offset
        picks = first_pick + jnp.arange(RECV, dtype=jnp.int32)
        usable = (picks >= 0) & (picks < own_count)
        bounded = jnp.clip(picks, 0, capacity - 1)
        result = []
        for member in members:
            blocks = member.reshape(capacity, BLOCK, member.shape[1])
            chosen = jnp.take(blocks, bounded, axis=0)
            kept = jnp.where(usable[:, None, None], chosen, jnp.zeros_like(chosen))
            result.append(kept.reshape(row_count, member.shape[1]))
        return tuple(result)

    members = (queries, keys, values)
    arranged = outgoing(members, 0)
    for distance in (1, -1):
        parts = outgoing(members, distance)
        arrived = jax.tree.map(
            lambda part, own: part.astype(own.dtype),
            shifted(shortened(parts), "dp", distance),
            parts,
        )
        arranged = tuple((held + extra for held, extra in zip(arranged, arrived)))
    query_rows, key_rows, value_rows = arranged
    earlier = []
    carried = (key_rows, value_rows)
    for hop_index in range(REACH):
        carried = shifted((carried[0], carried[1]), "dp", 1)
        earlier.append(carried)
    earlier = earlier[::-1]
    key_window = jnp.concatenate([piece[0] for piece in earlier] + [key_rows], axis=0)
    value_window = jnp.concatenate([piece[1] for piece in earlier] + [value_rows], axis=0)
    key_window, value_window = (key_window, value_window)
    reach_rows = REACH * row_count
    key_pos = base_row - reach_rows + jnp.arange(reach_rows + row_count, dtype=jnp.int32)
    query_pos = base_row + positions
    allowed = (key_pos[None, :] >= starts[:, None]) & (key_pos[None, :] <= query_pos[:, None])
    attn_out = attend(query_rows, key_window, value_window, allowed)
    token_score = jnp.dot(attn_out.astype(jnp.float32), reward_dir, precision=lax.Precision.HIGHEST)
    response_count = lax.axis_size("dp") * 2 // REACH
    matches = (
        segment_ids[:, None] == jnp.arange(response_count, dtype=jnp.int32)[None, :]
    ) & is_last[:, None]
    partial_rewards = jnp.sum(jnp.where(matches, token_score[:, None], 0.0), axis=0)
    rewards = lax.psum(partial_rewards, "dp")
    return (attn_out, rewards)


def solution(mesh):
    return jax.shard_map(
        shards,
        mesh=mesh,
        in_specs=(
            P(("groups", "dp"), None),
            P(("groups", "dp"), None),
            P(("groups", "dp"), None),
            P(("groups", "dp")),
            P(("groups", "dp")),
            P(),
        ),
        out_specs=(P(("groups", "dp"), None), P("groups")),
        check_vma=False,
    )
```

profile of v0, /device:TPU:0, one launch (start us, length us, event | category | flops | bytes accessed | tf_op | source)
XLA Modules:
  0.0 308.4 jit_solution(2750992244555226999)
XLA Ops:
  0.7 1.4 dynamic-slice
  2.0 1.9 fusion.63
  4.5 1.3 collective-permute-start.14
  5.9 0.8 slice_compare_fusion
  7.3 1.5 slice_dynamic-update-slice_fusion
  8.9 0.3 reduce-window.9
  9.6 0.8 dynamic-update-slice
  10.3 0.8 add_dynamic-update-slice_fusion
  11.2 15.8 %all-reduce.4 = (s32[16]{0:T(128)S(1)}, s32[16]{0:T(128)S(1)}, s32[16]{0:T(128)S(1)}, s32[16]{0:T(128)S(1)}) all-reduce(s32[16]{0:T(128)S(1)} %dynamic-update-slice, s32[16]{0:T(128)S(1)} %slice_dynamic-update-slice_fusion, s32[16]{0:T(128)S(1)} %get-tuple-element.116, ...), channel_id=2, replica_groups=mesh['groups'=2,'dp'=16] {'dp'}, use_global_device_ids=true, to_apply=%add | all-reduce | flops 64 | bytes 512
  27.0 0.6 gather_fusion.7
  27.6 1.7 gather_fusion.4
  29.4 0.8 copy.48
  30.3 5.7 %collective-permute-start.2 = (bf16[256,512]{0,1:T(8,128)(2,1)}, bf16[256,512]{0,1:T(8,128)(2,1)}, u32[]{:S(2)}, u32[]{:S(2)}) collective-permute-start(bf16[256,512]{0,1:T(8,128)(2,1)} %copy.48), channel_id=1, source_target_pairs={{0,1},{1,2},{2,3},{3,4},{4,5},{5,6},{6,7},{7,8},{8,9},{9,10},{10,1... | collective-permute-start | bytes 786440 | tf_op jit(solution)/shard_map/ppermute | solution.py:30
  36.2 11.8 %collective-permute-start.8 = (bf16[256,512]{0,1:T(8,128)(2,1)S(1)}, bf16[256,512]{0,1:T(8,128)(2,1)}, u32[]{:S(2)}, u32[]{:S(2)}) collective-permute-start(bf16[256,512]{0,1:T(8,128)(2,1)S(1)} %copy.52), channel_id=1, source_target_pairs={{0,1},{1,2},{2,3},{3,4},{4,5},{5,6},{6,7},{7,8},{8,9},{9,10},{10,1... | collective-permute-start | bytes 786440 | tf_op jit(solution)/shard_map/ppermute | solution.py:30
  48.0 0.6 gather_fusion.8
  48.6 1.7 gather_fusion.5
  50.4 0.8 copy.50
  51.3 1.3 collective-permute-start.3
  52.6 0.9 copy.54
  53.4 1.3 collective-permute-start.9
  54.7 3.5 %gather_fusion.2 = bf16[2,128,4096]{2,1,0:T(8,128)(2,1)S(1)} fusion(bf16[6,128,4096]{2,1,0:T(8,128)(2,1)} %bitcast.181, s32[1024]{0:T(1024)S(1)} %get-tuple-element.133), kind=kCustom, calls=%fused_computation.3.clone | custom fusion | bytes 4194312 | tf_op jit(solution)/shard_map/jit(_take)/gather | solution.py:114
  58.2 1.6 select_select_fusion
  59.8 0.6 gather_fusion.6
  60.4 1.7 gather_fusion.3
  62.1 3.5 %gather_fusion.1 = bf16[2,128,4096]{2,1,0:T(8,128)(2,1)S(1)} fusion(bf16[6,128,4096]{2,1,0:T(8,128)(2,1)} %bitcast.182, s32[1024]{0:T(1024)S(1)} %get-tuple-element.134), kind=kCustom, calls=%fused_computation.2.clone | custom fusion | bytes 4194312 | tf_op jit(solution)/shard_map/jit(_take)/gather | solution.py:114
  65.7 0.1 copy.53
  65.9 1.3 collective-permute-start.1
  67.2 1.1 add_add_fusion
  68.3 7.0 %collective-permute-start.10 = (bf16[256,512]{0,1:T(8,128)(2,1)S(1)}, bf16[256,512]{0,1:T(8,128)(2,1)S(1)}, u32[]{:S(2)}, u32[]{:S(2)}) collective-permute-start(bf16[256,512]{0,1:T(8,128)(2,1)S(1)} %add_add_fusion), channel_id=1, source_target_pairs={{0,1},{1,2},{2,3},{3,4},{4,5},{5,6},{6,7},{7,8},{8,9},{9,10},{10,1... | collective-permute-start | bytes 786440 | tf_op jit(solution)/shard_map/ppermute | solution.py:30
  75.2 1.6 select_select_fusion.1
  76.9 3.5 %gather_fusion = bf16[2,128,4096]{2,1,0:T(8,128)(2,1)S(1)} fusion(bf16[6,128,4096]{2,1,0:T(8,128)(2,1)} %bitcast.183, s32[1024]{0:T(1024)S(1)} %pad_clamp_fusion.2), kind=kCustom, calls=%fused_computation.clone | custom fusion | bytes 4194312 | tf_op jit(solution)/shard_map/jit(_take)/gather | solution.py:114
  80.3 0.1 copy.49
  80.5 12.0 %collective-permute-start = (bf16[256,4096]{1,0:T(8,128)(2,1)}, bf16[256,4096]{1,0:T(8,128)(2,1)}, u32[]{:S(2)}, u32[]{:S(2)}) collective-permute-start(bf16[256,4096]{1,0:T(8,128)(2,1)} %bitcast.185), channel_id=1, source_target_pairs={{0,1},{1,2},{2,3},{3,4},{4,5},{5,6},{6,7},{7,8},{8,9},{9,10},{10,1... | collective-permute-start | bytes 6291464 | tf_op jit(solution)/shard_map/ppermute | solution.py:30
  92.4 1.1 add_add_fusion.1
  93.5 4.9 %collective-permute-start.4 = (bf16[256,512]{0,1:T(8,128)(2,1)S(1)}, bf16[256,512]{0,1:T(8,128)(2,1)S(1)}, u32[]{:S(2)}, u32[]{:S(2)}) collective-permute-start(bf16[256,512]{0,1:T(8,128)(2,1)S(1)} %add_add_fusion.1), channel_id=1, source_target_pairs={{0,1},{1,2},{2,3},{3,4},{4,5},{5,6},{6,7},{7,8},{8,9},{9,10},{10,1... | collective-permute-start | bytes 786440 | tf_op jit(solution)/shard_map/ppermute | solution.py:30
  98.4 10.7 %collective-permute-start.11 = (bf16[256,512]{0,1:T(8,128)(2,1)S(1)}, bf16[256,512]{0,1:T(8,128)(2,1)S(1)}, u32[]{:S(2)}, u32[]{:S(2)}) collective-permute-start(bf16[256,512]{0,1:T(8,128)(2,1)S(1)} %collective-permute-done.10), channel_id=1, source_target_pairs={{0,1},{1,2},{2,3},{3,4},{4,5},{5,6},{6,7},{7,8},{8,9},{9,10},{10,1... | collective-permute-start | bytes 786440 | tf_op jit(solution)/shard_map/ppermute | solution.py:30
  109.1 1.6 select_select_fusion.2
  110.8 32.0 %collective-permute-start.5 = (bf16[256,512]{0,1:T(8,128)(2,1)S(1)}, bf16[256,512]{0,1:T(8,128)(2,1)S(1)}, u32[]{:S(2)}, u32[]{:S(2)}) collective-permute-start(bf16[256,512]{0,1:T(8,128)(2,1)S(1)} %collective-permute-done.4), channel_id=1, source_target_pairs={{0,1},{1,2},{2,3},{3,4},{4,5},{5,6},{6,7},{7,8},{8,9},{9,10},{10,1... | collective-permute-start | bytes 786440 | tf_op jit(solution)/shard_map/ppermute | solution.py:30
  142.8 4.4 %collective-permute-start.12 = (bf16[256,512]{0,1:T(8,128)(2,1)S(1)}, bf16[256,512]{0,1:T(8,128)(2,1)S(1)}, u32[]{:S(2)}, u32[]{:S(2)}) collective-permute-start(bf16[256,512]{0,1:T(8,128)(2,1)S(1)} %collective-permute-done.11), channel_id=1, source_target_pairs={{0,1},{1,2},{2,3},{3,4},{4,5},{5,6},{6,7},{7,8},{8,9},{9,10},{10,1... | collective-permute-start | bytes 786440 | tf_op jit(solution)/shard_map/ppermute | solution.py:30
  147.3 3.2 %collective-permute-start.6 = (bf16[256,512]{0,1:T(8,128)(2,1)S(1)}, bf16[256,512]{0,1:T(8,128)(2,1)S(1)}, u32[]{:S(2)}, u32[]{:S(2)}) collective-permute-start(bf16[256,512]{0,1:T(8,128)(2,1)S(1)} %collective-permute-done.5), channel_id=1, source_target_pairs={{0,1},{1,2},{2,3},{3,4},{4,5},{5,6},{6,7},{7,8},{8,9},{9,10},{10,1... | collective-permute-start | bytes 786440 | tf_op jit(solution)/shard_map/ppermute | solution.py:30
  150.5 4.4 %collective-permute-start.13 = (bf16[256,512]{0,1:T(8,128)(2,1)S(1)}, bf16[256,512]{0,1:T(8,128)(2,1)S(1)}, u32[]{:S(2)}, u32[]{:S(2)}) collective-permute-start(bf16[256,512]{0,1:T(8,128)(2,1)S(1)} %collective-permute-done.12), channel_id=1, source_target_pairs={{0,1},{1,2},{2,3},{3,4},{4,5},{5,6},{6,7},{7,8},{8,9},{9,10},{10,1... | collective-permute-start | bytes 786440 | tf_op jit(solution)/shard_map/ppermute | solution.py:30
  154.9 0.3 compare_and_fusion
  156.1 21.6 %collective-permute-start.7 = (bf16[256,512]{0,1:T(8,128)(2,1)S(1)}, bf16[256,512]{0,1:T(8,128)(2,1)S(1)}, u32[]{:S(2)}, u32[]{:S(2)}) collective-permute-start(bf16[256,512]{0,1:T(8,128)(2,1)S(1)} %collective-permute-done.6), channel_id=1, source_target_pairs={{0,1},{1,2},{2,3},{3,4},{4,5},{5,6},{6,7},{7,8},{8,9},{9,10},{10,1... | collective-permute-start | bytes 786440 | tf_op jit(solution)/shard_map/ppermute | solution.py:30
  177.8 1.1 constant_dynamic-update-slice_fusion.7
  179.1 0.3 copy-done.3
  179.4 2.5 fusion.24
  182.0 0.5 copy.68
  182.4 2.7 fusion.64
  185.1 5.6 %fusion.65 = (f32[2048]{0:T(1024)S(1)}, f32[2048,1280]{1,0:T(8,128)}) fusion(bf16[1280,4,128]{0,2,1:T(8,128)(2,1)S(1)} %bitcast.187, bf16[256,4,8,128]{3,2,1,0:T(8,128)(2,1)S(1)} %bitcast.177, pred[256,1280]{1,0:T(8,128)(4,1)S(1)} %compare_and_fusion), kind=kOutput, calls=%fused_computation.122 | convolution fusion | flops 678950912 | bytes 11673600 | tf_op jit(solution)/shard_map/dot_general | solution.py:48
  190.7 5.3 %fusion.66 = (f32[2048]{0:T(1024)S(1)}, f32[2048,1280]{1,0:T(8,128)}) fusion(bf16[1280,4,128]{0,2,1:T(8,128)(2,1)S(1)} %bitcast.188, bf16[256,4,8,128]{3,2,1,0:T(8,128)(2,1)S(1)} %bitcast.178, pred[256,1280]{1,0:T(8,128)(4,1)S(1)} %compare_and_fusion), kind=kOutput, calls=%fused_computation.123 | convolution fusion | flops 678950912 | bytes 11673600 | tf_op jit(solution)/shard_map/dot_general | solution.py:48
  196.0 5.1 %fusion.67 = (f32[2048]{0:T(1024)S(1)}, f32[2048,1280]{1,0:T(8,128)}) fusion(bf16[1280,4,128]{0,2,1:T(8,128)(2,1)S(1)} %bitcast.189, bf16[256,4,8,128]{3,2,1,0:T(8,128)(2,1)S(1)} %bitcast.179, pred[256,1280]{1,0:T(8,128)(4,1)S(1)} %compare_and_fusion), kind=kOutput, calls=%fused_computation.124 | convolution fusion | flops 678950912 | bytes 11673600 | tf_op jit(solution)/shard_map/dot_general | solution.py:48
  201.2 1.8 fusion.6
  203.1 5.7 %fusion.4 = f32[2048]{0:T(1024)S(1)} fusion(f32[2048,1280]{1,0:T(8,128)} %get-tuple-element.126, f32[2048]{0:T(1024)S(1)} %get-tuple-element.125), kind=kLoop, calls=%fused_computation.25 | loop fusion | flops 5240832 | bytes 10502144 | tf_op jit(solution)/shard_map/reduce_sum | solution.py:55
  208.9 6.0 %fusion.58 = bf16[256,1,8,128]{3,2,0,1:T(8,128)(2,1)S(1)} fusion(f32[2048,1280]{1,0:T(8,128)} %copy-done.2, f32[2048]{0:T(1024)S(1)} %get-tuple-element.123, f32[256,8]{1,0:T(8,128)S(1)} %div.49, bf16[1280,4,128]{0,2,1:T(8,128)(2,1)S(1)} %bitcast.199), kind=kOutput, calls=%fused_computation.59 | convolution fusion | flops 676855808 | bytes 11476992 | tf_op jit(solution)/shard_map/dot_general | solution.py:57
  214.9 6.0 %fusion.49 = bf16[256,1,8,128]{3,2,0,1:T(8,128)(2,1)S(1)} fusion(f32[2048,1280]{1,0:T(8,128)} %get-tuple-element.126, f32[2048]{0:T(1024)S(1)} %get-tuple-element.125, f32[256,8]{1,0:T(8,128)S(1)} %div.46, bf16[1280,4,128]{0,2,1:T(8,128)(2,1)S(1)} %bitcast.200), kind=kOutput, calls=%fused_computation.56 | convolution fusion | flops 676855808 | bytes 11476992 | tf_op jit(solution)/shard_map/dot_general | solution.py:57
  220.9 1.8 fusion.2
  222.8 5.8 %fusion.40 = bf16[256,1,8,128]{3,2,0,1:T(8,128)(2,1)S(1)} fusion(f32[2048,1280]{1,0:T(8,128)} %get-tuple-element.128, f32[2048]{0:T(1024)S(1)} %get-tuple-element.127, f32[256,8]{1,0:T(8,128)S(1)} %div.43, bf16[1280,4,128]{0,2,1:T(8,128)(2,1)S(1)} %bitcast.201), kind=kOutput, calls=%fused_computation.53 | convolution fusion | flops 676855808 | bytes 11476992 | tf_op jit(solution)/shard_map/dot_general | solution.py:57
  228.6 5.9 %fusion = f32[2048]{0:T(1024)S(1)} fusion(f32[2048,1280]{1,0:T(8,128)} %get-tuple-element.130, f32[2048]{0:T(1024)S(1)} %get-tuple-element.129), kind=kLoop, calls=%fused_computation.21 | loop fusion | flops 5240832 | bytes 10502144 | tf_op jit(solution)/shard_map/reduce_sum | solution.py:55
  234.6 5.8 %fusion.31 = bf16[256,1,8,128]{3,2,0,1:T(8,128)(2,1)S(1)} fusion(f32[2048,1280]{1,0:T(8,128)} %get-tuple-element.130, f32[2048]{0:T(1024)S(1)} %get-tuple-element.129, f32[256,8]{1,0:T(8,128)S(1)} %div.40, bf16[1280,4,128]{0,2,1:T(8,128)(2,1)S(1)} %bitcast.202), kind=kOutput, calls=%fused_computation.50 | convolution fusion | flops 676855808 | bytes 11476992 | tf_op jit(solution)/shard_map/dot_general | solution.py:57
  240.5 1.6 pad_maximum_fusion
  242.0 3.0 copy.62
  245.1 0.9 fusion.68
  246.1 2.9 copy.63
  249.0 59.4 %psum.7 = f32[8]{0:T(128)} all-reduce(f32[8]{0:T(128)S(1)} %select_reduce_fusion), channel_id=1, replica_groups=mesh['groups'=2,'dp'=16] {'dp'}, use_global_device_ids=true, to_apply=%region_13.16 | all-reduce | flops 8 | bytes 64 | tf_op jit(solution)/shard_map/psum | solution.py:150
  (84 shorter events, 2.0 us)
Async XLA Ops:
  0.6 26.4 %copy-start = (bf16[768,512]{1,0:T(8,128)(2,1)S(1)}, bf16[768,512]{1,0:T(8,128)(2,1)}, u32[]{:S(2)}) copy-start(bf16[768,512]{1,0:T(8,128)(2,1)} %param.14) | copy-start | bytes 2359300
  4.5 150.8 %collective-permute-start.14 = (s32[1]{0:T(128)}, s32[1]{0:T(128)}, u32[]{:S(2)}, u32[]{:S(2)}) collective-permute-start(s32[1]{0:T(128)} %add.136), channel_id=1, source_target_pairs={{1,0},{2,1},{3,2},{4,3},{5,4},{6,5},{7,6},{8,7},{9,8},{10,9},{11,1... | collective-permute-start | bytes 20 | tf_op jit(solution)/shard_map/ppermute | solution.py:30
  30.3 50.2 %collective-permute-start.2 = (bf16[256,512]{0,1:T(8,128)(2,1)}, bf16[256,512]{0,1:T(8,128)(2,1)}, u32[]{:S(2)}, u32[]{:S(2)}) collective-permute-start(bf16[256,512]{0,1:T(8,128)(2,1)} %copy.48), channel_id=1, source_target_pairs={{0,1},{1,2},{2,3},{3,4},{4,5},{5,6},{6,7},{7,8},{8,9},{9,10},{10,1... | collective-permute-start | bytes 786440 | tf_op jit(solution)/shard_map/ppermute | solution.py:30
  36.2 29.7 %collective-permute-start.8 = (bf16[256,512]{0,1:T(8,128)(2,1)S(1)}, bf16[256,512]{0,1:T(8,128)(2,1)}, u32[]{:S(2)}, u32[]{:S(2)}) collective-permute-start(bf16[256,512]{0,1:T(8,128)(2,1)S(1)} %copy.52), channel_id=1, source_target_pairs={{0,1},{1,2},{2,3},{3,4},{4,5},{5,6},{6,7},{7,8},{8,9},{9,10},{10,1... | collective-permute-start | bytes 786440 | tf_op jit(solution)/shard_map/ppermute | solution.py:30
  51.3 41.2 %collective-permute-start.3 = (bf16[256,512]{0,1:T(8,128)(2,1)}, bf16[256,512]{0,1:T(8,128)(2,1)}, u32[]{:S(2)}, u32[]{:S(2)}) collective-permute-start(bf16[256,512]{0,1:T(8,128)(2,1)} %copy.50), channel_id=1, source_target_pairs={{1,0},{2,1},{3,2},{4,3},{5,4},{6,5},{7,6},{8,7},{9,8},{10,9},{11,1... | collective-permute-start | bytes 786440 | tf_op jit(solution)/shard_map/ppermute | solution.py:30
  53.4 13.8 %collective-permute-start.9 = (bf16[256,512]{0,1:T(8,128)(2,1)}, bf16[256,512]{0,1:T(8,128)(2,1)}, u32[]{:S(2)}, u32[]{:S(2)}) collective-permute-start(bf16[256,512]{0,1:T(8,128)(2,1)} %copy.54), channel_id=1, source_target_pairs={{1,0},{2,1},{3,2},{4,3},{5,4},{6,5},{7,6},{8,7},{9,8},{10,9},{11,1... | collective-permute-start | bytes 786440 | tf_op jit(solution)/shard_map/ppermute | solution.py:30
  65.9 113.2 %collective-permute-start.1 = (bf16[256,4096]{1,0:T(8,128)(2,1)}, bf16[256,4096]{1,0:T(8,128)(2,1)}, u32[]{:S(2)}, u32[]{:S(2)}) collective-permute-start(bf16[256,4096]{1,0:T(8,128)(2,1)} %bitcast.184), channel_id=1, source_target_pairs={{1,0},{2,1},{3,2},{4,3},{5,4},{6,5},{7,6},{8,7},{9,8},{10,9},{11,1... | collective-permute-start | bytes 6291464 | tf_op jit(solution)/shard_map/ppermute | solution.py:30
  68.3 30.2 %collective-permute-start.10 = (bf16[256,512]{0,1:T(8,128)(2,1)S(1)}, bf16[256,512]{0,1:T(8,128)(2,1)S(1)}, u32[]{:S(2)}, u32[]{:S(2)}) collective-permute-start(bf16[256,512]{0,1:T(8,128)(2,1)S(1)} %add_add_fusion), channel_id=1, source_target_pairs={{0,1},{1,2},{2,3},{3,4},{4,5},{5,6},{6,7},{7,8},{8,9},{9,10},{10,1... | collective-permute-start | bytes 786440 | tf_op jit(solution)/shard_map/ppermute | solution.py:30
  80.5 98.7 %collective-permute-start = (bf16[256,4096]{1,0:T(8,128)(2,1)}, bf16[256,4096]{1,0:T(8,128)(2,1)}, u32[]{:S(2)}, u32[]{:S(2)}) collective-permute-start(bf16[256,4096]{1,0:T(8,128)(2,1)} %bitcast.185), channel_id=1, source_target_pairs={{0,1},{1,2},{2,3},{3,4},{4,5},{5,6},{6,7},{7,8},{8,9},{9,10},{10,1... | collective-permute-start | bytes 6291464 | tf_op jit(solution)/shard_map/ppermute | solution.py:30
  93.5 53.7 %copy-start.9 = (s32[256]{0:T(256)S(1)}, s32[256]{0:T(256)}, u32[]{:S(2)}) copy-start(s32[256]{0:T(256)} %param.16) | copy-start | bytes 3076
  93.5 17.2 %collective-permute-start.4 = (bf16[256,512]{0,1:T(8,128)(2,1)S(1)}, bf16[256,512]{0,1:T(8,128)(2,1)S(1)}, u32[]{:S(2)}, u32[]{:S(2)}) collective-permute-start(bf16[256,512]{0,1:T(8,128)(2,1)S(1)} %add_add_fusion.1), channel_id=1, source_target_pairs={{0,1},{1,2},{2,3},{3,4},{4,5},{5,6},{6,7},{7,8},{8,9},{9,10},{10,1... | collective-permute-start | bytes 786440 | tf_op jit(solution)/shard_map/ppermute | solution.py:30
  98.4 44.4 %collective-permute-start.11 = (bf16[256,512]{0,1:T(8,128)(2,1)S(1)}, bf16[256,512]{0,1:T(8,128)(2,1)S(1)}, u32[]{:S(2)}, u32[]{:S(2)}) collective-permute-start(bf16[256,512]{0,1:T(8,128)(2,1)S(1)} %collective-permute-done.10), channel_id=1, source_target_pairs={{0,1},{1,2},{2,3},{3,4},{4,5},{5,6},{6,7},{7,8},{8,9},{9,10},{10,1... | collective-permute-start | bytes 786440 | tf_op jit(solution)/shard_map/ppermute | solution.py:30
  110.8 39.7 %copy-start.4 = (bf16[256,512]{0,1:T(8,128)(2,1)}, bf16[256,512]{0,1:T(8,128)(2,1)S(1)}, u32[]{:S(2)}) copy-start(bf16[256,512]{0,1:T(8,128)(2,1)S(1)} %collective-permute-done.4) | copy-start | bytes 786436
  110.8 36.5 %collective-permute-start.5 = (bf16[256,512]{0,1:T(8,128)(2,1)S(1)}, bf16[256,512]{0,1:T(8,128)(2,1)S(1)}, u32[]{:S(2)}, u32[]{:S(2)}) collective-permute-start(bf16[256,512]{0,1:T(8,128)(2,1)S(1)} %collective-permute-done.4), channel_id=1, source_target_pairs={{0,1},{1,2},{2,3},{3,4},{4,5},{5,6},{6,7},{7,8},{8,9},{9,10},{10,1... | collective-permute-start | bytes 786440 | tf_op jit(solution)/shard_map/ppermute | solution.py:30
  142.8 7.7 %copy-start.6 = (bf16[256,512]{0,1:T(8,128)(2,1)}, bf16[256,512]{0,1:T(8,128)(2,1)S(1)}, u32[]{:S(2)}) copy-start(bf16[256,512]{0,1:T(8,128)(2,1)S(1)} %collective-permute-done.11) | copy-start | bytes 786436
  142.8 7.7 %collective-permute-start.12 = (bf16[256,512]{0,1:T(8,128)(2,1)S(1)}, bf16[256,512]{0,1:T(8,128)(2,1)S(1)}, u32[]{:S(2)}, u32[]{:S(2)}) collective-permute-start(bf16[256,512]{0,1:T(8,128)(2,1)S(1)} %collective-permute-done.11), channel_id=1, source_target_pairs={{0,1},{1,2},{2,3},{3,4},{4,5},{5,6},{6,7},{7,8},{8,9},{9,10},{10,1... | collective-permute-start | bytes 786440 | tf_op jit(solution)/shard_map/ppermute | solution.py:30
  147.3 8.8 %collective-permute-start.6 = (bf16[256,512]{0,1:T(8,128)(2,1)S(1)}, bf16[256,512]{0,1:T(8,128)(2,1)S(1)}, u32[]{:S(2)}, u32[]{:S(2)}) collective-permute-start(bf16[256,512]{0,1:T(8,128)(2,1)S(1)} %collective-permute-done.5), channel_id=1, source_target_pairs={{0,1},{1,2},{2,3},{3,4},{4,5},{5,6},{6,7},{7,8},{8,9},{9,10},{10,1... | collective-permute-start | bytes 786440 | tf_op jit(solution)/shard_map/ppermute | solution.py:30
  150.5 27.2 %collective-permute-start.13 = (bf16[256,512]{0,1:T(8,128)(2,1)S(1)}, bf16[256,512]{0,1:T(8,128)(2,1)S(1)}, u32[]{:S(2)}, u32[]{:S(2)}) collective-permute-start(bf16[256,512]{0,1:T(8,128)(2,1)S(1)} %collective-permute-done.12), channel_id=1, source_target_pairs={{0,1},{1,2},{2,3},{3,4},{4,5},{5,6},{6,7},{7,8},{8,9},{9,10},{10,1... | collective-permute-start | bytes 786440 | tf_op jit(solution)/shard_map/ppermute | solution.py:30
  156.1 23.0 %copy-start.5 = (bf16[256,512]{0,1:T(8,128)(2,1)S(1)}, bf16[256,512]{0,1:T(8,128)(2,1)}, u32[]{:S(2)}) copy-start(bf16[256,512]{0,1:T(8,128)(2,1)} %copy-done.4) | copy-start | bytes 786436
  156.1 22.9 %collective-permute-start.7 = (bf16[256,512]{0,1:T(8,128)(2,1)S(1)}, bf16[256,512]{0,1:T(8,128)(2,1)S(1)}, u32[]{:S(2)}, u32[]{:S(2)}) collective-permute-start(bf16[256,512]{0,1:T(8,128)(2,1)S(1)} %collective-permute-done.6), channel_id=1, source_target_pairs={{0,1},{1,2},{2,3},{3,4},{4,5},{5,6},{6,7},{7,8},{8,9},{9,10},{10,1... | collective-permute-start | bytes 786440 | tf_op jit(solution)/shard_map/ppermute | solution.py:30
  177.8 1.7 copy-start.3
  178.9 35.9 %copy-start.7 = (bf16[1280,512]{0,1:T(8,128)(2,1)}, bf16[1280,512]{0,1:T(8,128)(2,1)S(1)}, u32[]{:S(2)}) copy-start(bf16[1280,512]{0,1:T(8,128)(2,1)S(1)} %constant_dynamic-update-slice_fusion.5) | copy-start | bytes 3932164
  185.1 16.1 %copy-start.2 = (f32[2048,1280]{1,0:T(8,128)}, f32[2048,1280]{1,0:T(8,128)S(1)}, u32[]{:S(2)}) copy-start(f32[2048,1280]{1,0:T(8,128)S(1)} %get-tuple-element.124) | copy-start | bytes 31457284
  208.8 12.0 %slice-start = ((s8[10485760]{0:T(1024)(128)(4,1)}), s8[4194304]{0:T(1024)(128)(4,1)S(1)}, s32[]{:S(2)}) async-start(s8[10485760]{0:T(1024)(128)(4,1)} %bitcast.172), calls=%async_computation | async-start | bytes 8388608
  208.8 12.0 %slice-start.1 = ((s8[10485760]{0:T(1024)(128)(4,1)}), s8[4194304]{0:T(1024)(128)(4,1)S(1)}, s32[]{:S(2)}) async-start(s8[10485760]{0:T(1024)(128)(4,1)} %bitcast.172), calls=%async_computation.1 | async-start | bytes 8388608
  214.8 6.0 %slice-start.2 = ((s8[10485760]{0:T(1024)(128)(4,1)}), s8[2097152]{0:T(1024)(128)(4,1)S(1)}, s32[]{:S(2)}) async-start(s8[10485760]{0:T(1024)(128)(4,1)} %bitcast.172), calls=%async_computation.2 | async-start | bytes 4194304
  220.9 1.9 copy-start.8
  242.0 3.0 copy-start.10
  246.0 62.4 %copy-start.1 = (bf16[768,512]{1,0:T(8,128)(2,1)S(1)}, bf16[768,512]{1,0:T(8,128)(2,1)}, u32[]{:S(2)}) copy-start(bf16[768,512]{1,0:T(8,128)(2,1)} %param.14) | copy-start | bytes 2359300
where the time goes:
time: 310 us; the launch traced here: 308 us
  starting transfers between devices  123 us (40%)
  blocking collectives  75.2 us (24%)
  matrix products  43.2 us (14%)
  local copies, waits for them, and re-layouts  34.3 us (11%)
  other arithmetic  29.4 us (9%)
  between operations  3.36 us (1%)
    ppermute x15, starting transfers between devices, shifted(): return lax.ppermute(block, axis, route)  123 us
    psum x1, blocking collectives, shards(): rewards = lax.psum(partial_rewards, 'dp')  59.4 us
    dot_general x4, matrix products, attend(): jnp.dot(soft_weights, value_heads[:, head_index], preferred_element_type=...  23.6 us
    dot_general x4, matrix products, attend(): jnp.dot(query_head, key_heads[:, head_index].T, preferred_element_type=jn...  18.7 us
    gather x9, local copies, waits for them, and re-layouts, outgoing(): chosen = jnp.take(blocks, bounded, axis=0)  17.2 us
    unnamed x1, blocking collectives  15.8 us
    reduce_sum x4, other arithmetic, attend(): totals = jnp.sum(raised, axis=-1)  15.1 us
    unnamed x45, local copies, waits for them, and re-layouts  8.63 us
  transfers between devices with their start and end apart: 15, of which 0 were waited for; matrix products, arithmetic and copies ran while one was open for 11% of the time, Pallas kernels for 0%

commit v1 on v0

v1 whole, which is shorter than its diff:
```python
import functools

import jax
import jax.numpy as jnp
from jax import lax
from jax.experimental import pallas as pl
from jax.experimental.pallas import tpu as pltpu
from jax.sharding import PartitionSpec as P

D_HEAD = 128
HEADS = 32
KV_HEADS = 4
BLOCK = 128
REACH = 4
LANES = 128
PER_GROUP = HEADS // KV_HEADS
LOG2E = 1.4426950408889634
MASKED = -1e30


def kernel(
    n, q_hbm, k_hbm, v_hbm, meta_ref, cols_ref, dir_ref, out_ref, rew_ref,
    qv, kv, vv, meta_all, send_q, recv_q, send_kv, recv_kv, win, qp, bias, score,
    part, part_all,
    load_sem, meta_send, meta_recv, kv_send, kv_recv, q_send, q_recv,
    win_send, win_recv, part_send, part_recv,
):
    me = lax.axis_index("dp")
    core = lax.rem(me, 2)
    partner = me + 1 - 2 * core
    rows = cols_ref.shape[1]
    recv = rows // BLOCK
    cap = qv.shape[0]
    width = PER_GROUP * D_HEAD
    kv_width = KV_HEADS * D_HEAD
    id_rows = rows // LANES

    loads = [
        pltpu.make_async_copy(k_hbm, kv, load_sem.at[0]),
        pltpu.make_async_copy(v_hbm, vv, load_sem.at[1]),
        pltpu.make_async_copy(q_hbm, qv, load_sem.at[2]),
    ]
    for load in loads:
        load.start()

    for pad in list(range(REACH)) + [n + REACH]:
        meta_all[pad] = jnp.full((8, LANES), -1, jnp.int32)
    meta_all[pl.ds(me + REACH, 1)] = meta_ref[...][None]
    for distance in (2, 4):
        @pl.when(me < distance)
        def _():
            win[:, pl.ds((4 - distance) * rows, 2 * rows), :] = jnp.zeros(
                (KV_HEADS, 2 * rows, 2 * D_HEAD), win.dtype
            )
    score[...] = jnp.zeros_like(score)

    barrier = pltpu.get_barrier_semaphore()

    def greet(i, carry):
        pl.semaphore_signal(
            barrier, inc=1, device_id={"dp": lax.rem(me + i, n)},
            device_id_type=pl.DeviceIdType.MESH,
        )
        return carry

    lax.fori_loop(1, n, greet, 0)
    pl.semaphore_wait(barrier, n - 1)

    def remote(src, dst, send_sem, recv_sem, rank):
        return pltpu.make_async_remote_copy(
            src_ref=src, dst_ref=dst, send_sem=send_sem, recv_sem=recv_sem,
            device_id={"dp": rank}, device_id_type=pl.DeviceIdType.MESH,
        )

    def tell_all(src, table, shift, send_sem, recv_sem):
        def begin(i, carry):
            remote(src, table.at[me + shift], send_sem.at[i], recv_sem.at[i],
                   lax.rem(me + i, n)).start()
            return carry

        lax.fori_loop(1, n, begin, 0)

    def hear_all(src, table, shift, send_sem, recv_sem):
        def finish(i, carry):
            came = lax.rem(me + n - i, n)
            remote(src, table.at[came + shift], send_sem.at[i], recv_sem.at[i],
                   lax.rem(me + i, n)).wait()
            return carry

        lax.fori_loop(1, n, finish, 0)

    tell_all(meta_ref, meta_all, REACH, meta_send, meta_recv)
    hear_all(meta_ref, meta_all, REACH, meta_send, meta_recv)

    counts = meta_all[REACH:REACH + n, id_rows, :]
    rank_index = lax.broadcasted_iota(jnp.int32, (n, LANES), 0)
    offset = jnp.sum(jnp.where(rank_index < me, counts, 0), axis=0, keepdims=True)[0, 0]
    count = meta_ref[id_rows:id_rows + 1, :][0, 0]

    def pick(distance, slot):
        return jnp.clip((me + distance) * recv + slot - offset, 0, cap - 1)

    routes = ((0, 1, me + 1, me < n - 1, me > 0), (1, -1, me - 1, me > 0, me < n - 1))

    def both(start_or_wait):
        for d, distance, rank, sends, receives in routes:
            start_or_wait(d, rank, sends, receives)

    for load in loads[:2]:
        load.wait()
    for d, distance, rank, sends, receives in routes:
        for slot in range(recv):
            at = pl.ds(slot * BLOCK, BLOCK)
            chosen = pick(distance, slot)
            send_kv[d, at, :kv_width] = kv[chosen]
            send_kv[d, at, kv_width:] = vv[chosen]

        @pl.when(sends)
        def _():
            remote(send_kv.at[d], recv_kv.at[d], kv_send.at[d], kv_recv.at[d], rank).start()

    loads[2].wait()

    def prepare_q(g):
        for d, distance, rank, sends, receives in routes:
            for slot in range(recv):
                send_q[d, g, pl.ds(slot * BLOCK, BLOCK), :] = qv[
                    pick(distance, slot), :, g * width:(g + 1) * width
                ]

    def q_copy(d, g, rank):
        return remote(send_q.at[d, g], recv_q.at[d, g], q_send.at[d, g], q_recv.at[d, g], rank)

    def start_q(g):
        for d, distance, rank, sends, receives in routes:
            @pl.when(sends)
            def _():
                q_copy(d, g, rank).start()

    prepare_q(0)
    start_q(0)
    prepare_q(1)

    row_at = lax.broadcasted_iota(jnp.int32, (rows, LANES), 0)
    lane_at = lax.broadcasted_iota(jnp.int32, (rows, LANES), 1)
    ids = cols_ref[0]
    for chunk in range((REACH + 1) * id_rows):
        key_ids = meta_all[pl.ds(me + chunk // id_rows, 1)][0, chunk % id_rows:chunk % id_rows + 1, :]
        key_at = lane_at + (chunk * LANES - REACH * rows)
        bias[:, chunk * LANES:(chunk + 1) * LANES] = jnp.where(
            (ids == key_ids) & (key_at <= row_at), 0.0, MASKED
        )

    for d, distance, rank, sends, receives in routes:
        @pl.when(receives)
        def _():
            remote(send_kv.at[d], recv_kv.at[d], kv_send.at[d], kv_recv.at[d], rank).wait_recv()

    def source(slot):
        block = me * recv + slot
        return block < offset, block >= offset + count

    for slot in range(recv):
        before, after = source(slot)
        at = pl.ds(slot * BLOCK, BLOCK)
        home = pl.ds((4 + core) * rows + slot * BLOCK, BLOCK)
        chosen = pick(0, slot)
        for part_at, held in ((0, kv), (1, vv)):
            columns = slice(part_at * kv_width, (part_at + 1) * kv_width)
            own = held[chosen]
            got = jnp.where(before, recv_kv[0, at, columns], own)
            got = jnp.where(after, recv_kv[1, at, columns], got)
            for g in range(KV_HEADS):
                win[g, home, part_at * D_HEAD:(part_at + 1) * D_HEAD] = got[
                    :, g * D_HEAD:(g + 1) * D_HEAD
                ]

    def win_copy(hop, g, place, rank):
        here = win.at[g, pl.ds((place + core) * rows, rows), :]
        dst = place - hop if hop in (2, 4) else place
        there = win.at[g, pl.ds((dst + core) * rows, rows), :]
        index = {2: 0, 4: 1}.get(hop, 2 + place // 2)
        return remote(here, there, win_send.at[index, g], win_recv.at[index, g], rank)

    for g in range(KV_HEADS):
        for hop in (2, 4):
            @pl.when(me + hop < n)
            def _():
                win_copy(hop, g, 4, me + hop).start()
        win_copy(0, g, 4, partner).start()

    start_q(1)
    for g in range(2, KV_HEADS):
        prepare_q(g)

    for g in range(KV_HEADS):
        for hop in (2, 4):
            @pl.when(me >= hop)
            def _():
                win_copy(hop, g, 4, me + hop).wait_recv()
                win_copy(0, g, 4 - hop, partner).start()

    span = (REACH + 1) * rows - (recv - 1) * BLOCK
    scale = D_HEAD ** -0.5 * LOG2E

    for g in range(KV_HEADS):
        for d, distance, rank, sends, receives in routes:
            @pl.when(receives)
            def _():
                q_copy(d, g, rank).wait_recv()
        if g + 2 < KV_HEADS:
            start_q(g + 2)
        for slot in range(recv):
            before, after = source(slot)
            at = pl.ds(slot * BLOCK, BLOCK)
            chosen = pick(0, slot)
            for h in range(PER_GROUP):
                columns = slice(h * D_HEAD, (h + 1) * D_HEAD)
                own = qv[chosen, :, g * width + h * D_HEAD:g * width + (h + 1) * D_HEAD]
                got = jnp.where(before, recv_q[0, g, at, columns], own)
                got = jnp.where(after, recv_q[1, g, at, columns], got)
                qp[h, at, :] = got
        win_copy(0, g, 4, partner).wait_recv()
        for hop in (2, 4):
            @pl.when(me >= hop)
            def _():
                win_copy(0, g, 4 - hop, partner).wait_recv()

        for slot in range(recv):
            start = pl.multiple_of(core * rows + slot * BLOCK, BLOCK)
            at = slice(slot * BLOCK, (slot + 1) * BLOCK)

            def heads(pair, carry):
                keys = win[g, pl.ds(start, span), :D_HEAD]
                values = win[g, pl.ds(start, span), D_HEAD:]
                query = qp[pl.ds(pair * 2, 2), at, :].reshape(2 * BLOCK, D_HEAD)
                logits = lax.dot_general(
                    query, keys, (((1,), (1,)), ((), ())), preferred_element_type=jnp.float32
                )
                mask = bias[at, slot * BLOCK:slot * BLOCK + span]
                logits = logits.reshape(2, BLOCK, span) * scale + mask[None]
                top = jnp.max(logits, axis=-1, keepdims=True)
                raised = jnp.exp2(logits - top)
                totals = jnp.sum(raised, axis=-1, keepdims=True)
                weights = raised.astype(jnp.bfloat16).reshape(2 * BLOCK, span)
                head_out = jnp.dot(weights, values, preferred_element_type=jnp.float32)
                head_out = (head_out.reshape(2, BLOCK, D_HEAD) / totals).astype(jnp.bfloat16)
                for i in range(2):
                    head = g * PER_GROUP + pair * 2 + i
                    column = pl.multiple_of(head * D_HEAD, D_HEAD)
                    out_ref[at, pl.ds(column, D_HEAD)] = head_out[i]
                    score[at, :] += head_out[i].astype(jnp.float32) * dir_ref[pl.ds(head, 1), :]
                return carry

            lax.fori_loop(0, PER_GROUP // 2, heads, 0)

    next_first = meta_all[pl.ds(me + REACH + 1, 1)][0, 0:1, 0:1]
    following = jnp.where(row_at == rows - 1, next_first, cols_ref[1])
    token_score = jnp.sum(score[...], axis=-1, keepdims=True)
    chosen = (ids == lane_at) & (ids != following)
    partial = jnp.sum(jnp.where(chosen, token_score, 0.0), axis=0, keepdims=True)
    part[...] = jnp.broadcast_to(partial, part.shape)
    part_all[pl.ds(me, 1)] = part[...][None]
    tell_all(part, part_all, 0, part_send, part_recv)

    for d, distance, rank, sends, receives in routes:
        @pl.when(sends)
        def _():
            remote(send_kv.at[d], recv_kv.at[d], kv_send.at[d], kv_recv.at[d], rank).wait_send()
            for g in range(KV_HEADS):
                q_copy(d, g, rank).wait_send()
    for g in range(KV_HEADS):
        win_copy(0, g, 4, partner).wait_send()
        for hop in (2, 4):
            @pl.when(me + hop < n)
            def _():
                win_copy(hop, g, 4, me + hop).wait_send()

            @pl.when(me >= hop)
            def _():
                win_copy(0, g, 4 - hop, partner).wait_send()

    hear_all(part, part_all, 0, part_send, part_recv)
    rew_ref[...] = jnp.sum(part_all[...], axis=0)


def shards(queries, keys, values, block_counts, segment_ids, reward_dir):
    n = lax.axis_size("dp")
    rows = segment_ids.shape[0]
    cap = queries.shape[0] // BLOCK
    kv_width = keys.shape[1]
    width = PER_GROUP * D_HEAD
    id_rows = rows // LANES
    meta = jnp.concatenate([
        segment_ids.reshape(id_rows, LANES),
        jnp.broadcast_to(block_counts[:, None], (8 - id_rows, LANES)),
    ])
    following = jnp.concatenate([segment_ids[1:], segment_ids[-1:]])
    cols = jnp.broadcast_to(jnp.stack([segment_ids, following])[:, :, None], (2, rows, LANES))
    vmem = pl.BlockSpec(memory_space=pltpu.VMEM)
    hbm = pl.BlockSpec(memory_space=pl.ANY)
    dma = pltpu.SemaphoreType.DMA
    bf16 = jnp.bfloat16
    attn_out, rewards = pl.pallas_call(
        functools.partial(kernel, n),
        out_shape=(
            jax.ShapeDtypeStruct((rows, HEADS * D_HEAD), bf16),
            jax.ShapeDtypeStruct((8, LANES), jnp.float32),
        ),
        in_specs=[hbm, hbm, hbm, vmem, vmem, vmem],
        out_specs=(vmem, vmem),
        scratch_shapes=[
            pltpu.VMEM((cap, BLOCK, HEADS * D_HEAD), bf16),
            pltpu.VMEM((cap, BLOCK, kv_width), bf16),
            pltpu.VMEM((cap, BLOCK, kv_width), bf16),
            pltpu.VMEM((n + REACH + 1, 8, LANES), jnp.int32),
            pltpu.VMEM((2, KV_HEADS, rows, width), bf16),
            pltpu.VMEM((2, KV_HEADS, rows, width), bf16),
            pltpu.VMEM((2, rows, 2 * kv_width), bf16),
            pltpu.VMEM((2, rows, 2 * kv_width), bf16),
            pltpu.VMEM((KV_HEADS, (REACH + 2) * rows, 2 * D_HEAD), bf16),
            pltpu.VMEM((PER_GROUP, rows, D_HEAD), bf16),
            pltpu.VMEM((rows, (REACH + 1) * rows), jnp.float32),
            pltpu.VMEM((rows, LANES), jnp.float32),
            pltpu.VMEM((8, LANES), jnp.float32),
            pltpu.VMEM((n, 8, LANES), jnp.float32),
            dma((3,)),
            dma((n,)), dma((n,)),
            dma((2,)), dma((2,)),
            dma((2, KV_HEADS)), dma((2, KV_HEADS)),
            dma((5, KV_HEADS)), dma((5, KV_HEADS)),
            dma((n,)), dma((n,)),
        ],
        compiler_params=pltpu.CompilerParams(
            collective_id=0, has_side_effects=True, vmem_limit_bytes=56 * 1024 * 1024
        ),
    )(
        queries.reshape(cap, BLOCK, -1), keys.reshape(cap, BLOCK, -1),
        values.reshape(cap, BLOCK, -1), meta, cols, reward_dir.reshape(HEADS, D_HEAD),
    )
    response_count = n * 2 // REACH
    return attn_out, rewards[0, :response_count]


def solution(mesh):
    return jax.shard_map(
        shards,
        mesh=mesh,
        in_specs=(
            P(("groups", "dp"), None),
            P(("groups", "dp"), None),
            P(("groups", "dp"), None),
            P(("groups", "dp")),
            P(("groups", "dp")),
            P(),
        ),
        out_specs=(P(("groups", "dp"), None), P("groups")),
        check_vma=False,
    )
```

time: 310 us -> 107 us (0.35)
  starting transfers between devices: 123 us -> 0 us
  Pallas kernels: 0 us -> 95.2 us
  blocking collectives: 75.2 us -> 0 us
  matrix products: 43.2 us -> 0 us
  other arithmetic: 29.4 us -> 1.4 us
  local copies, waits for them, and re-layouts: 34.3 us -> 8.44 us
    ppermute x15 -> x0, starting transfers between devices: 123 us -> none  [shifted(): return lax.ppermute(block, axis, route)]
    pallas_call x0 -> x1, Pallas kernels: none -> 95.2 us  [shards(): pl.pallas_call(functools.partial(kernel, n), out_shape=(jax.ShapeDtypeStr...]
    psum x1 -> x0, blocking collectives: 59.4 us -> none  [shards(): rewards = lax.psum(partial_rewards, 'dp')]
    dot_general x9 -> x0, matrix products: 43.2 us -> none  [the longest x4 23.6 us: attend(): jnp.dot(soft_weights, value_heads[:, head_index], preferred_element_type=...]
    gather x9 -> x0, local copies, waits for them, and re-layouts: 17.2 us -> none  [outgoing(): chosen = jnp.take(blocks, bounded, axis=0)]
    unnamed x1 -> x0, blocking collectives: 15.8 us -> none
    reduce_sum x5 -> x0, other arithmetic: 15.2 us -> none  [the longest x4 15.1 us: attend(): totals = jnp.sum(raised, axis=-1)]
    unnamed x45 -> x1, local copies, waits for them, and re-layouts: 8.63 us -> 3.13 us
  transfers between devices with their start and end apart: 15 -> 0, of which waited for: 0 -> 0; matrix products, arithmetic and copies ran while one was open for 11% -> 0% of each run, Pallas kernels for 0% -> 0%
where the time goes in v1:
time: 107 us; the launch traced here: 106 us
  Pallas kernels  95.2 us (89%)
  local copies, waits for them, and re-layouts  8.44 us (8%)
  other arithmetic  1.4 us (1%)
  between operations  1.29 us (1%)
    pallas_call x1, Pallas kernels, shards(): pl.pallas_call(functools.partial(kernel, n), out_shape=(jax.ShapeDtypeStr...  95.2 us
    unnamed x1, local copies, waits for them, and re-layouts  3.13 us

profile of v1, /device:TPU:0, one launch (start us, length us, event | category | flops | bytes accessed | tf_op | source)
XLA Modules:
  0.0 106.4 jit_solution(1121540420678014789)
XLA Ops:
  1.3 1.3 %slice.10 = s32[1]{0:T(128)} slice(s32[256]{0:T(256)} %param.10), slice={[255:256]} | slice | bytes 8 | tf_op jit(solution)/shard_map/slice | solution.py:298
  2.5 0.7 slice.9
  3.3 0.7 pad_add_fusion.1
  4.0 0.7 pad_add_fusion
  4.7 1.3 %concatenate.6.meta_ref = s32[8,128]{1,0:T(8,128)} pad(s32[2,128]{1,0:T(2,128)} %bitcast.16, s32[]{:T(128)} %bitcast.10), padding=0_6x0_0 | pad | bytes 5124 | tf_op jit(solution)/shard_map/concatenate | solution.py:294
  6.0 0.8 broadcast_in_dim.5.cols_ref
  6.8 95.2 %shard_map.77 = (bf16[256,4096]{1,0:T(8,128)(2,1)}, f32[8,128]{1,0:T(8,128)}) custom-call(bf16[6,128,4096]{2,1,0:T(8,128)(2,1)} %bitcast.11, bf16[6,128,512]{2,1,0:T(8,128)(2,1)} %bitcast.12, bf16[6,128,512]{2,1,0:T(8,128)(2,1)} %bitcast.13, s32[8,128]{1,0:T(8,128)} %concatenate.6.meta_ref, s32[2,256,128]{2,1,0:T(8,128)} %broadcast_in_dim.5.cols_ref, ...), custom_call_target="tpu_custom_call" | custom-call | tf_op jit(solution)/shard_map/pallas_call | solution.py:304
  102.0 1.2 %slice_bitcast_fusion = f32[8]{0:T(128)} fusion(f32[8,128]{1,0:T(8,128)} %get-tuple-element.5), kind=kLoop, calls=%fused_computation.2 | loop fusion | bytes 64 | tf_op jit(solution)/shard_map/squeeze | solution.py:342
  103.2 3.1 %copy.10 = bf16[256,4096]{1,0:T(8,128)(2,1)} copy(bf16[256,4096]{1,0:T(8,128)(2,1)} %get-tuple-element.8) | data formatting | bytes 4194304

commit v2 on v1

--- a/solution.py
+++ b/solution.py
@@ -14,13 +14,16 @@
 REACH = 4
 LANES = 128
 PER_GROUP = HEADS // KV_HEADS
+PER_CHUNK = 4
+CHUNKS = HEADS // PER_CHUNK
+AHEAD = 3
 LOG2E = 1.4426950408889634
 MASKED = -1e30
 
 
 def kernel(
-    n, q_hbm, k_hbm, v_hbm, meta_ref, cols_ref, dir_ref, out_ref, rew_ref,
-    qv, kv, vv, meta_all, send_q, recv_q, send_kv, recv_kv, win, qp, bias, score,
+    n, q_hbm, k_hbm, v_hbm, count_ref, ids_ref, dir_ref, out_ref, rew_ref,
+    meta_ref, qv, kv, vv, meta_all, send_q, recv_q, send_kv, recv_kv, win, qp, bias, score,
     part, part_all,
     load_sem, meta_send, meta_recv, kv_send, kv_recv, q_send, q_recv,
     win_send, win_recv, part_send, part_recv,
@@ -28,10 +31,10 @@
     me = lax.axis_index("dp")
     core = lax.rem(me, 2)
     partner = me + 1 - 2 * core
-    rows = cols_ref.shape[1]
+    rows = ids_ref.shape[1]
     recv = rows // BLOCK
     cap = qv.shape[0]
-    width = PER_GROUP * D_HEAD
+    width = PER_CHUNK * D_HEAD
     kv_width = KV_HEADS * D_HEAD
     id_rows = rows // LANES
 
@@ -43,6 +46,10 @@
     for load in loads:
         load.start()
 
+    count = count_ref[0]
+    meta_ref[...] = jnp.full((8, LANES), count, jnp.int32)
+    for i in range(id_rows):
+        meta_ref[i:i + 1, :] = ids_ref[:, i * LANES:(i + 1) * LANES]
     for pad in list(range(REACH)) + [n + REACH]:
         meta_all[pad] = jnp.full((8, LANES), -1, jnp.int32)
     meta_all[pl.ds(me + REACH, 1)] = meta_ref[...][None]
@@ -95,7 +102,6 @@
     counts = meta_all[REACH:REACH + n, id_rows, :]
     rank_index = lax.broadcasted_iota(jnp.int32, (n, LANES), 0)
     offset = jnp.sum(jnp.where(rank_index < me, counts, 0), axis=0, keepdims=True)[0, 0]
-    count = meta_ref[id_rows:id_rows + 1, :][0, 0]
 
     def pick(distance, slot):
         return jnp.clip((me + distance) * recv + slot - offset, 0, cap - 1)
@@ -139,11 +145,15 @@
 
     prepare_q(0)
     start_q(0)
-    prepare_q(1)
+    for c in range(1, CHUNKS):
+        prepare_q(c)
 
     row_at = lax.broadcasted_iota(jnp.int32, (rows, LANES), 0)
     lane_at = lax.broadcasted_iota(jnp.int32, (rows, LANES), 1)
-    ids = cols_ref[0]
+    ids = jnp.concatenate([
+        jnp.transpose(jnp.broadcast_to(ids_ref[:, i * LANES:(i + 1) * LANES], (LANES, LANES)))
+        for i in range(id_rows)
+    ])
     for chunk in range((REACH + 1) * id_rows):
         key_ids = meta_all[pl.ds(me + chunk // id_rows, 1)][0, chunk % id_rows:chunk % id_rows + 1, :]
         key_at = lane_at + (chunk * LANES - REACH * rows)
@@ -182,60 +192,65 @@
         index = {2: 0, 4: 1}.get(hop, 2 + place // 2)
         return remote(here, there, win_send.at[index, g], win_recv.at[index, g], rank)
 
-    for g in range(KV_HEADS):
+    def start_win(g):
         for hop in (2, 4):
             @pl.when(me + hop < n)
             def _():
                 win_copy(hop, g, 4, me + hop).start()
         win_copy(0, g, 4, partner).start()
 
-    start_q(1)
-    for g in range(2, KV_HEADS):
-        prepare_q(g)
-
-    for g in range(KV_HEADS):
+    def forward_win(g):
         for hop in (2, 4):
             @pl.when(me >= hop)
             def _():
                 win_copy(hop, g, 4, me + hop).wait_recv()
                 win_copy(0, g, 4 - hop, partner).start()
 
+    start_win(0)
+    start_q(1)
+    start_win(1)
+    start_q(2)
+    forward_win(0)
+
     span = (REACH + 1) * rows - (recv - 1) * BLOCK
     scale = D_HEAD ** -0.5 * LOG2E
 
-    for g in range(KV_HEADS):
+    for c in range(CHUNKS):
+        g = c * PER_CHUNK // PER_GROUP
+        opens = c * PER_CHUNK % PER_GROUP == 0
         for d, distance, rank, sends, receives in routes:
             @pl.when(receives)
             def _():
-                q_copy(d, g, rank).wait_recv()
-        if g + 2 < KV_HEADS:
-            start_q(g + 2)
+                q_copy(d, c, rank).wait_recv()
+        if c + AHEAD < CHUNKS:
+            start_q(c + AHEAD)
         for slot in range(recv):
             before, after = source(slot)
             at = pl.ds(slot * BLOCK, BLOCK)
             chosen = pick(0, slot)
-            for h in range(PER_GROUP):
+            for h in range(PER_CHUNK):
                 columns = slice(h * D_HEAD, (h + 1) * D_HEAD)
-                own = qv[chosen, :, g * width + h * D_HEAD:g * width + (h + 1) * D_HEAD]
-                got = jnp.where(before, recv_q[0, g, at, columns], own)
-                got = jnp.where(after, recv_q[1, g, at, columns], got)
+                own = qv[chosen, :, c * width + h * D_HEAD:c * width + (h + 1) * D_HEAD]
+                got = jnp.where(before, recv_q[0, c, at, columns], own)
+                got = jnp.where(after, recv_q[1, c, at, columns], got)
                 qp[h, at, :] = got
-        win_copy(0, g, 4, partner).wait_recv()
-        for hop in (2, 4):
-            @pl.when(me >= hop)
-            def _():
-                win_copy(0, g, 4 - hop, partner).wait_recv()
+        if opens:
+            win_copy(0, g, 4, partner).wait_recv()
+            for hop in (2, 4):
+                @pl.when(me >= hop)
+                def _():
+                    win_copy(0, g, 4 - hop, partner).wait_recv()
 
         for slot in range(recv):
             start = pl.multiple_of(core * rows + slot * BLOCK, BLOCK)
             at = slice(slot * BLOCK, (slot + 1) * BLOCK)
-
-            def heads(pair, carry):
-                keys = win[g, pl.ds(start, span), :D_HEAD]
-                values = win[g, pl.ds(start, span), D_HEAD:]
-                query = qp[pl.ds(pair * 2, 2), at, :].reshape(2 * BLOCK, D_HEAD)
+            keys = win.at[g, pl.ds(start, span), :D_HEAD]
+            values = win.at[g, pl.ds(start, span), D_HEAD:]
+            for pair in range(PER_CHUNK // 2):
+                query = qp[pair * 2:pair * 2 + 2, at, :].reshape(2 * BLOCK, D_HEAD)
                 logits = lax.dot_general(
-                    query, keys, (((1,), (1,)), ((), ())), preferred_element_type=jnp.float32
+                    query, keys[...], (((1,), (1,)), ((), ())),
+                    preferred_element_type=jnp.float32,
                 )
                 mask = bias[at, slot * BLOCK:slot * BLOCK + span]
                 logits = logits.reshape(2, BLOCK, span) * scale + mask[None]
@@ -243,19 +258,20 @@
                 raised = jnp.exp2(logits - top)
                 totals = jnp.sum(raised, axis=-1, keepdims=True)
                 weights = raised.astype(jnp.bfloat16).reshape(2 * BLOCK, span)
-                head_out = jnp.dot(weights, values, preferred_element_type=jnp.float32)
+                head_out = jnp.dot(weights, values[...], preferred_element_type=jnp.float32)
                 head_out = (head_out.reshape(2, BLOCK, D_HEAD) / totals).astype(jnp.bfloat16)
                 for i in range(2):
-                    head = g * PER_GROUP + pair * 2 + i
-                    column = pl.multiple_of(head * D_HEAD, D_HEAD)
-                    out_ref[at, pl.ds(column, D_HEAD)] = head_out[i]
-                    score[at, :] += head_out[i].astype(jnp.float32) * dir_ref[pl.ds(head, 1), :]
-                return carry
-
-            lax.fori_loop(0, PER_GROUP // 2, heads, 0)
+                    head = c * PER_CHUNK + pair * 2 + i
+                    out_ref[at, head * D_HEAD:(head + 1) * D_HEAD] = head_out[i]
+                    score[at, :] += head_out[i].astype(jnp.float32) * dir_ref[head:head + 1, :]
+
+        if opens and g + 1 < KV_HEADS:
+            forward_win(g + 1)
+            if g + 2 < KV_HEADS:
+                start_win(g + 2)
 
     next_first = meta_all[pl.ds(me + REACH + 1, 1)][0, 0:1, 0:1]
-    following = jnp.where(row_at == rows - 1, next_first, cols_ref[1])
+    following = jnp.where(row_at == rows - 1, next_first, pltpu.roll(ids, rows - 1, 0))
     token_score = jnp.sum(score[...], axis=-1, keepdims=True)
     chosen = (ids == lane_at) & (ids != following)
     partial = jnp.sum(jnp.where(chosen, token_score, 0.0), axis=0, keepdims=True)
@@ -267,8 +283,8 @@
         @pl.when(sends)
         def _():
             remote(send_kv.at[d], recv_kv.at[d], kv_send.at[d], kv_recv.at[d], rank).wait_send()
-            for g in range(KV_HEADS):
-                q_copy(d, g, rank).wait_send()
+            for c in range(CHUNKS):
+                q_copy(d, c, rank).wait_send()
     for g in range(KV_HEADS):
         win_copy(0, g, 4, partner).wait_send()
         for hop in (2, 4):
@@ -281,7 +297,7 @@
                 win_copy(0, g, 4 - hop, partner).wait_send()
 
     hear_all(part, part_all, 0, part_send, part_recv)
-    rew_ref[...] = jnp.sum(part_all[...], axis=0)
+    rew_ref[...] = jnp.sum(part_all[...], axis=0)[0:1, :rew_ref.shape[1]]
 
 
 def shards(queries, keys, values, block_counts, segment_ids, reward_dir):
@@ -289,14 +305,8 @@
     rows = segment_ids.shape[0]
     cap = queries.shape[0] // BLOCK
     kv_width = keys.shape[1]
-    width = PER_GROUP * D_HEAD
-    id_rows = rows // LANES
-    meta = jnp.concatenate([
-        segment_ids.reshape(id_rows, LANES),
-        jnp.broadcast_to(block_counts[:, None], (8 - id_rows, LANES)),
-    ])
-    following = jnp.concatenate([segment_ids[1:], segment_ids[-1:]])
-    cols = jnp.broadcast_to(jnp.stack([segment_ids, following])[:, :, None], (2, rows, LANES))
+    width = PER_CHUNK * D_HEAD
+    response_count = n * 2 // REACH
     vmem = pl.BlockSpec(memory_space=pltpu.VMEM)
     hbm = pl.BlockSpec(memory_space=pl.ANY)
     dma = pltpu.SemaphoreType.DMA
@@ -305,21 +315,22 @@
         functools.partial(kernel, n),
         out_shape=(
             jax.ShapeDtypeStruct((rows, HEADS * D_HEAD), bf16),
-            jax.ShapeDtypeStruct((8, LANES), jnp.float32),
+            jax.ShapeDtypeStruct((1, response_count), jnp.float32),
         ),
-        in_specs=[hbm, hbm, hbm, vmem, vmem, vmem],
+        in_specs=[hbm, hbm, hbm, pl.BlockSpec(memory_space=pltpu.SMEM), vmem, vmem],
         out_specs=(vmem, vmem),
         scratch_shapes=[
+            pltpu.VMEM((8, LANES), jnp.int32),
             pltpu.VMEM((cap, BLOCK, HEADS * D_HEAD), bf16),
             pltpu.VMEM((cap, BLOCK, kv_width), bf16),
             pltpu.VMEM((cap, BLOCK, kv_width), bf16),
             pltpu.VMEM((n + REACH + 1, 8, LANES), jnp.int32),
-            pltpu.VMEM((2, KV_HEADS, rows, width), bf16),
-            pltpu.VMEM((2, KV_HEADS, rows, width), bf16),
+            pltpu.VMEM((2, CHUNKS, rows, width), bf16),
+            pltpu.VMEM((2, CHUNKS, rows, width), bf16),
             pltpu.VMEM((2, rows, 2 * kv_width), bf16),
             pltpu.VMEM((2, rows, 2 * kv_width), bf16),
             pltpu.VMEM((KV_HEADS, (REACH + 2) * rows, 2 * D_HEAD), bf16),
-            pltpu.VMEM((PER_GROUP, rows, D_HEAD), bf16),
+            pltpu.VMEM((PER_CHUNK, rows, D_HEAD), bf16),
             pltpu.VMEM((rows, (REACH + 1) * rows), jnp.float32),
             pltpu.VMEM((rows, LANES), jnp.float32),
             pltpu.VMEM((8, LANES), jnp.float32),
@@ -327,7 +338,7 @@
             dma((3,)),
             dma((n,)), dma((n,)),
             dma((2,)), dma((2,)),
-            dma((2, KV_HEADS)), dma((2, KV_HEADS)),
+            dma((2, CHUNKS)), dma((2, CHUNKS)),
             dma((5, KV_HEADS)), dma((5, KV_HEADS)),
             dma((n,)), dma((n,)),
         ],
@@ -336,10 +347,9 @@
         ),
     )(
         queries.reshape(cap, BLOCK, -1), keys.reshape(cap, BLOCK, -1),
-        values.reshape(cap, BLOCK, -1), meta, cols, reward_dir.reshape(HEADS, D_HEAD),
+        values.reshape(cap, BLOCK, -1), block_counts, segment_ids.reshape(1, rows), reward_dir.reshape(HEADS, D_HEAD),
     )
-    response_count = n * 2 // REACH
-    return attn_out, rewards[0, :response_count]
+    return attn_out, rewards.reshape(response_count)
 
 
 def solution(mesh):

time: 107 us -> 96.8 us (0.905)
  local copies, waits for them, and re-layouts: 8.44 us -> 3.65 us
  Pallas kernels: 95.2 us -> 91.6 us
  other arithmetic: 1.4 us -> 0 us
    pallas_call x1, Pallas kernels: 95.2 us -> 91.6 us  [shards(): pl.pallas_call(functools.partial(kernel, n), out_shape=(jax.ShapeDtypeStr...]
    slice x2 -> x0, local copies, waits for them, and re-layouts: 2.01 us -> none  [shards(): following = jnp.concatenate([segment_ids[1:], segment_ids[-1:]])]
    concatenate x1 -> x0, local copies, waits for them, and re-layouts: 1.27 us -> none  [shards(): jnp.concatenate([segment_ids.reshape(id_rows, LANES), jnp.broadcast_to(bl...]
    squeeze x1 -> x0, local copies, waits for them, and re-layouts: 1.19 us -> none  [shards(): return (attn_out, rewards[0, :response_count])]
    unnamed x1 -> x4, local copies, waits for them, and re-layouts: 3.13 us -> 3.65 us
where the time goes in v2:
time: 96.8 us; the launch traced here: 96.6 us
  Pallas kernels  91.6 us (95%)
  local copies, waits for them, and re-layouts  3.65 us (4%)
  between operations  1.29 us (1%)
    pallas_call x1, Pallas kernels, shards(): pl.pallas_call(functools.partial(kernel, n), out_shape=(jax.ShapeDtypeStr...  91.6 us
    unnamed x4, local copies, waits for them, and re-layouts  3.65 us

profile of v2, /device:TPU:0, one launch (start us, length us, event | category | flops | bytes accessed | tf_op | source)
XLA Modules:
  0.0 96.6 jit_solution(8874337429004838196)
XLA Ops:
  1.3 91.6 %shard_map.77 = (bf16[256,4096]{1,0:T(8,128)(2,1)}, f32[1,8]{1,0:T(1,128)}) custom-call(bf16[6,128,4096]{2,1,0:T(8,128)(2,1)} %bitcast.6, bf16[6,128,512]{2,1,0:T(8,128)(2,1)} %bitcast.7, bf16[6,128,512]{2,1,0:T(8,128)(2,1)} %bitcast.8, s32[1]{0:T(128)S(6)} %copy.10.count_ref, s32[1,256]{1,0:T(1,128)} %bitcast.10, f32[32,128]{1,0:T(8,128)} %bitcast.9), custom_call_target="tpu_custom_call" | custom-call | tf_op jit(solution)/shard_map/pallas_call | solution.py:314
  92.9 0.0 copy-start
  92.9 3.1 %copy.11 = bf16[256,4096]{1,0:T(8,128)(2,1)} copy(bf16[256,4096]{1,0:T(8,128)(2,1)} %get-tuple-element.8) | data formatting | bytes 4194304
  96.0 0.0 copy-done
  96.0 0.5 copy.12
Async XLA Ops:
  92.9 3.1 %copy-start = (f32[1,8]{1,0:T(1,128)S(1)}, f32[1,8]{1,0:T(1,128)}, u32[]{:S(2)}) copy-start(f32[1,8]{1,0:T(1,128)} %get-tuple-element.5) | copy-start | bytes 100

commit v3 on v2

--- a/solution.py
+++ b/solution.py
@@ -16,7 +16,8 @@
 PER_GROUP = HEADS // KV_HEADS
 PER_CHUNK = 4
 CHUNKS = HEADS // PER_CHUNK
-AHEAD = 3
+AHEAD = 4
+PLANE = 4
 LOG2E = 1.4426950408889634
 MASKED = -1e30
 
@@ -24,9 +25,9 @@
 def kernel(
     n, q_hbm, k_hbm, v_hbm, count_ref, ids_ref, dir_ref, out_ref, rew_ref,
     meta_ref, qv, kv, vv, meta_all, send_q, recv_q, send_kv, recv_kv, win, qp, bias, score,
-    part, part_all,
+    part, part_all, relay, out_buf,
     load_sem, meta_send, meta_recv, kv_send, kv_recv, q_send, q_recv,
-    win_send, win_recv, part_send, part_recv,
+    win_send, win_recv, part_send, part_recv, relay_send, relay_recv, out_sem,
 ):
     me = lax.axis_index("dp")
     core = lax.rem(me, 2)
@@ -137,9 +138,48 @@
     def q_copy(d, g, rank):
         return remote(send_q.at[d, g], recv_q.at[d, g], q_send.at[d, g], q_recv.at[d, g], rank)
 
+    place = lax.rem(me, PLANE)
+    plane = me // PLANE
+    planes = n // PLANE
+
+    def early(border, c):
+        return (c * 3 % CHUNKS) * planes < (planes - 1 - border) * CHUNKS
+
+    def crosses(d):
+        return place == (PLANE - 1 if d == 0 else 0)
+
+    def relay_out(d, c):
+        border = plane if d == 0 else plane - 1
+        near, far = (-2, 4) if d == 0 else (-4, 2)
+        rank = jnp.where(early(border, c), me + near, me + far)
+        return remote(send_q.at[d, c], relay.at[c], q_send.at[d, c], relay_recv.at[c], rank)
+
+    relay_d = 1 - lax.rem(place, 2)
+    relay_to = jnp.where(place < 2, me + 3, me - 3)
+    relay_border = jnp.where(place < 2, plane, plane - 1)
+    relay_open = (relay_border >= 0) & (relay_border < planes - 1)
+
+    def relays(c):
+        return relay_open & (early(relay_border, c) == (place < 2))
+
+    def relay_on(c):
+        return remote(
+            relay.at[c], recv_q.at[relay_d, c], relay_send.at[c], q_recv.at[relay_d, c], relay_to
+        )
+
+    def forward_q(c):
+        @pl.when(relays(c))
+        def _():
+            remote(relay.at[c], relay.at[c], relay_send.at[c], relay_recv.at[c], relay_to).wait_recv()
+            relay_on(c).start()
+
     def start_q(g):
         for d, distance, rank, sends, receives in routes:
-            @pl.when(sends)
+            @pl.when(sends & crosses(d))
+            def _():
+                relay_out(d, g).start()
+
+            @pl.when(sends & jnp.logical_not(crosses(d)))
             def _():
                 q_copy(d, g, rank).start()
 
@@ -208,12 +248,19 @@
 
     start_win(0)
     start_q(1)
+    forward_q(0)
     start_win(1)
     start_q(2)
     forward_win(0)
+    start_q(3)
+    forward_q(1)
 
     span = (REACH + 1) * rows - (recv - 1) * BLOCK
     scale = D_HEAD ** -0.5 * LOG2E
+
+    def out_copy(c):
+        columns = pl.ds(c * width, width)
+        return pltpu.make_async_copy(out_buf.at[:, columns], out_ref.at[:, columns], out_sem.at[c])
 
     for c in range(CHUNKS):
         g = c * PER_CHUNK // PER_GROUP
@@ -242,6 +289,8 @@
                     win_copy(0, g, 4 - hop, partner).wait_recv()
 
         for slot in range(recv):
+            if slot == 1 and c + 2 < CHUNKS:
+                forward_q(c + 2)
             start = pl.multiple_of(core * rows + slot * BLOCK, BLOCK)
             at = slice(slot * BLOCK, (slot + 1) * BLOCK)
             keys = win.at[g, pl.ds(start, span), :D_HEAD]
@@ -262,9 +311,10 @@
                 head_out = (head_out.reshape(2, BLOCK, D_HEAD) / totals).astype(jnp.bfloat16)
                 for i in range(2):
                     head = c * PER_CHUNK + pair * 2 + i
-                    out_ref[at, head * D_HEAD:(head + 1) * D_HEAD] = head_out[i]
+                    out_buf[at, head * D_HEAD:(head + 1) * D_HEAD] = head_out[i]
                     score[at, :] += head_out[i].astype(jnp.float32) * dir_ref[head:head + 1, :]
 
+        out_copy(c).start()
         if opens and g + 1 < KV_HEADS:
             forward_win(g + 1)
             if g + 2 < KV_HEADS:
@@ -296,6 +346,12 @@
             def _():
                 win_copy(0, g, 4 - hop, partner).wait_send()
 
+    for c in range(CHUNKS):
+        @pl.when(relays(c))
+        def _():
+            relay_on(c).wait_send()
+
+        out_copy(c).wait()
     hear_all(part, part_all, 0, part_send, part_recv)
     rew_ref[...] = jnp.sum(part_all[...], axis=0)[0:1, :rew_ref.shape[1]]
 
@@ -318,7 +374,7 @@
             jax.ShapeDtypeStruct((1, response_count), jnp.float32),
         ),
         in_specs=[hbm, hbm, hbm, pl.BlockSpec(memory_space=pltpu.SMEM), vmem, vmem],
-        out_specs=(vmem, vmem),
+        out_specs=(hbm, vmem),
         scratch_shapes=[
             pltpu.VMEM((8, LANES), jnp.int32),
             pltpu.VMEM((cap, BLOCK, HEADS * D_HEAD), bf16),
@@ -335,12 +391,15 @@
             pltpu.VMEM((rows, LANES), jnp.float32),
             pltpu.VMEM((8, LANES), jnp.float32),
             pltpu.VMEM((n, 8, LANES), jnp.float32),
+            pltpu.VMEM((CHUNKS, rows, width), bf16),
+            pltpu.VMEM((rows, HEADS * D_HEAD), bf16),
             dma((3,)),
             dma((n,)), dma((n,)),
             dma((2,)), dma((2,)),
             dma((2, CHUNKS)), dma((2, CHUNKS)),
             dma((5, KV_HEADS)), dma((5, KV_HEADS)),
             dma((n,)), dma((n,)),
+            dma((CHUNKS,)), dma((CHUNKS,)), dma((CHUNKS,)),
         ],
         compiler_params=pltpu.CompilerParams(
             collective_id=0, has_side_effects=True, vmem_limit_bytes=56 * 1024 * 1024

time: 96.8 us -> 90.4 us (0.934)
  Pallas kernels: 91.6 us -> 85.2 us
    pallas_call x1, Pallas kernels: 91.6 us -> 85.2 us  [shards(): pl.pallas_call(functools.partial(kernel, n), out_shape=(jax.ShapeDtypeStr...]
where the time goes in v3:
time: 90.4 us; the launch traced here: 90.1 us
  Pallas kernels  85.2 us (94%)
  local copies, waits for them, and re-layouts  3.65 us (4%)
  between operations  1.29 us (1%)
    pallas_call x1, Pallas kernels, shards(): pl.pallas_call(functools.partial(kernel, n), out_shape=(jax.ShapeDtypeStr...  85.2 us
    unnamed x4, local copies, waits for them, and re-layouts  3.65 us

profile of v3, /device:TPU:0, one launch (start us, length us, event | category | flops | bytes accessed | tf_op | source)
XLA Modules:
  0.0 90.1 jit_solution(606948286555117071)
XLA Ops:
  1.3 85.2 %shard_map.77 = (bf16[256,4096]{1,0:T(8,128)(2,1)}, f32[1,8]{1,0:T(1,128)}) custom-call(bf16[6,128,4096]{2,1,0:T(8,128)(2,1)} %bitcast.6, bf16[6,128,512]{2,1,0:T(8,128)(2,1)} %bitcast.7, bf16[6,128,512]{2,1,0:T(8,128)(2,1)} %bitcast.8, s32[1]{0:T(128)S(6)} %copy.10.count_ref, s32[1,256]{1,0:T(1,128)} %bitcast.10, f32[32,128]{1,0:T(8,128)} %bitcast.9), custom_call_target="tpu_custom_call" | custom-call | tf_op jit(solution)/shard_map/pallas_call | solution.py:370
  86.5 0.0 copy-start
  86.5 3.1 %copy.11 = bf16[256,4096]{1,0:T(8,128)(2,1)} copy(bf16[256,4096]{1,0:T(8,128)(2,1)} %get-tuple-element.8) | data formatting | bytes 4194304
  89.6 0.0 copy-done
  89.6 0.5 copy.12
Async XLA Ops:
  86.5 3.1 %copy-start = (f32[1,8]{1,0:T(1,128)S(1)}, f32[1,8]{1,0:T(1,128)}, u32[]{:S(2)}) copy-start(f32[1,8]{1,0:T(1,128)} %get-tuple-element.5) | copy-start | bytes 100

commit v4 on v3

--- a/solution.py
+++ b/solution.py
@@ -14,9 +14,11 @@
 REACH = 4
 LANES = 128
 PER_GROUP = HEADS // KV_HEADS
-PER_CHUNK = 4
+PER_CHUNK = 2
 CHUNKS = HEADS // PER_CHUNK
-AHEAD = 4
+AHEAD = 8
+LEAD = 4
+PARTS = 8
 PLANE = 4
 LOG2E = 1.4426950408889634
 MASKED = -1e30
@@ -248,12 +250,18 @@
 
     start_win(0)
     start_q(1)
+    start_q(2)
+    start_q(3)
     forward_q(0)
     start_win(1)
-    start_q(2)
+    start_q(4)
+    start_q(5)
     forward_win(0)
-    start_q(3)
     forward_q(1)
+    for c in range(6, AHEAD):
+        start_q(c)
+    for c in range(2, LEAD):
+        forward_q(c)
 
     span = (REACH + 1) * rows - (recv - 1) * BLOCK
     scale = D_HEAD ** -0.5 * LOG2E
@@ -289,8 +297,8 @@
                     win_copy(0, g, 4 - hop, partner).wait_recv()
 
         for slot in range(recv):
-            if slot == 1 and c + 2 < CHUNKS:
-                forward_q(c + 2)
+            if slot == 1 and c + LEAD < CHUNKS:
+                forward_q(c + LEAD)
             start = pl.multiple_of(core * rows + slot * BLOCK, BLOCK)
             at = slice(slot * BLOCK, (slot + 1) * BLOCK)
             keys = win.at[g, pl.ds(start, span), :D_HEAD]
@@ -354,6 +362,26 @@
         out_copy(c).wait()
     hear_all(part, part_all, 0, part_send, part_recv)
     rew_ref[...] = jnp.sum(part_all[...], axis=0)[0:1, :rew_ref.shape[1]]
+
+
+def handed_on(source, target, held, in_sem, out_sem):
+    step = source.shape[0] // PARTS
+    parts = [pl.ds(i * step, step) for i in range(PARTS)]
+    reads = [
+        pltpu.make_async_copy(source.at[at], held.at[at], in_sem.at[i])
+        for i, at in enumerate(parts)
+    ]
+    writes = [
+        pltpu.make_async_copy(held.at[at], target.at[at], out_sem.at[i])
+        for i, at in enumerate(parts)
+    ]
+    for read in reads:
+        read.start()
+    for read, write in zip(reads, writes):
+        read.wait()
+        write.start()
+    for write in writes:
+        write.wait()
 
 
 def shards(queries, keys, values, block_counts, segment_ids, reward_dir):
@@ -408,6 +436,14 @@
         queries.reshape(cap, BLOCK, -1), keys.reshape(cap, BLOCK, -1),
         values.reshape(cap, BLOCK, -1), block_counts, segment_ids.reshape(1, rows), reward_dir.reshape(HEADS, D_HEAD),
     )
+    attn_out = pl.pallas_call(
+        handed_on,
+        out_shape=jax.ShapeDtypeStruct(attn_out.shape, bf16),
+        in_specs=[hbm],
+        out_specs=hbm,
+        scratch_shapes=[pltpu.VMEM(attn_out.shape, bf16), dma((PARTS,)), dma((PARTS,))],
+        compiler_params=pltpu.CompilerParams(vmem_limit_bytes=56 * 1024 * 1024),
+    )(attn_out)
     return attn_out, rewards.reshape(response_count)
 
 

time: 90.4 us -> 91.7 us (1.014)
  Pallas kernels: 85.2 us -> 89.6 us
  local copies, waits for them, and re-layouts: 3.65 us -> 0.52 us
    unnamed x4 -> x3, local copies, waits for them, and re-layouts: 3.65 us -> 0.52 us
    pallas_call x0 -> x1, Pallas kernels: none -> 2.39 us  [shards(): pl.pallas_call(handed_on, out_shape=jax.ShapeDtypeStruct(attn_out.shape,...]
    pallas_call x1, Pallas kernels: 85.2 us -> 87.2 us  [shards(): pl.pallas_call(functools.partial(kernel, n), out_shape=(jax.ShapeDtypeStr...]
where the time goes in v4:
time: 91.7 us; the launch traced here: 91.5 us
  Pallas kernels  89.6 us (98%)
  between operations  1.31 us (1%)
    pallas_call x1, Pallas kernels, shards(): pl.pallas_call(functools.partial(kernel, n), out_shape=(jax.ShapeDtypeStr...  87.2 us
    pallas_call x1, Pallas kernels, shards(): pl.pallas_call(handed_on, out_shape=jax.ShapeDtypeStruct(attn_out.shape,...  2.39 us

profile of v4, /device:TPU:0, one launch (start us, length us, event | category | flops | bytes accessed | tf_op | source)
XLA Modules:
  0.0 91.5 jit_solution(3153986602725545175)
XLA Ops:
  1.3 87.2 %shard_map.77 = (bf16[256,4096]{1,0:T(8,128)(2,1)}, f32[1,8]{1,0:T(1,128)}) custom-call(bf16[6,128,4096]{2,1,0:T(8,128)(2,1)} %bitcast.6, bf16[6,128,512]{2,1,0:T(8,128)(2,1)} %bitcast.7, bf16[6,128,512]{2,1,0:T(8,128)(2,1)} %bitcast.8, s32[1]{0:T(128)S(6)} %copy.9.count_ref, s32[1,256]{1,0:T(1,128)} %bitcast.10, f32[32,128]{1,0:T(8,128)} %bitcast.9), custom_call_target="tpu_custom_call" | custom-call | tf_op jit(solution)/shard_map/pallas_call | solution.py:398
  88.5 0.0 copy-start
  88.5 2.4 %shard_map.78 = bf16[256,4096]{1,0:T(8,128)(2,1)} custom-call(bf16[256,4096]{1,0:T(8,128)(2,1)} %get-tuple-element.4.source), custom_call_target="tpu_custom_call" | custom-call | tf_op jit(solution)/shard_map/pallas_call | solution.py:439
  90.9 0.0 copy-done
  90.9 0.5 copy.10
Async XLA Ops:
  88.5 2.4 %copy-start = (f32[1,8]{1,0:T(1,128)S(1)}, f32[1,8]{1,0:T(1,128)}, u32[]{:S(2)}) copy-start(f32[1,8]{1,0:T(1,128)} %get-tuple-element.5) | copy-start | bytes 100

commit v5 on v4

--- a/solution.py
+++ b/solution.py
@@ -14,10 +14,10 @@
 REACH = 4
 LANES = 128
 PER_GROUP = HEADS // KV_HEADS
-PER_CHUNK = 2
+PER_CHUNK = 4
 CHUNKS = HEADS // PER_CHUNK
-AHEAD = 8
-LEAD = 4
+AHEAD = 4
+LEAD = 2
 PARTS = 8
 PLANE = 4
 LOG2E = 1.4426950408889634
@@ -250,18 +250,12 @@
 
     start_win(0)
     start_q(1)
-    start_q(2)
-    start_q(3)
     forward_q(0)
     start_win(1)
-    start_q(4)
-    start_q(5)
+    start_q(2)
     forward_win(0)
+    start_q(3)
     forward_q(1)
-    for c in range(6, AHEAD):
-        start_q(c)
-    for c in range(2, LEAD):
-        forward_q(c)
 
     span = (REACH + 1) * rows - (recv - 1) * BLOCK
     scale = D_HEAD ** -0.5 * LOG2E

time: 91.7 us -> 89.7 us (0.978)
  Pallas kernels: 89.6 us -> 87.6 us
    pallas_call x1, Pallas kernels: 87.2 us -> 85.2 us  [shards(): pl.pallas_call(functools.partial(kernel, n), out_shape=(jax.ShapeDtypeStr...]
where the time goes in v5:
time: 89.7 us; the launch traced here: 89.4 us
  Pallas kernels  87.6 us (98%)
  between operations  1.31 us (1%)
    pallas_call x1, Pallas kernels, shards(): pl.pallas_call(functools.partial(kernel, n), out_shape=(jax.ShapeDtypeStr...  85.2 us
    pallas_call x1, Pallas kernels, shards(): pl.pallas_call(handed_on, out_shape=jax.ShapeDtypeStruct(attn_out.shape,...  2.39 us

profile of v5, /device:TPU:0, one launch (start us, length us, event | category | flops | bytes accessed | tf_op | source)
XLA Modules:
  0.0 89.4 jit_solution(10611546854275852471)
XLA Ops:
  1.3 85.2 %shard_map.77 = (bf16[256,4096]{1,0:T(8,128)(2,1)}, f32[1,8]{1,0:T(1,128)}) custom-call(bf16[6,128,4096]{2,1,0:T(8,128)(2,1)} %bitcast.6, bf16[6,128,512]{2,1,0:T(8,128)(2,1)} %bitcast.7, bf16[6,128,512]{2,1,0:T(8,128)(2,1)} %bitcast.8, s32[1]{0:T(128)S(6)} %copy.9.count_ref, s32[1,256]{1,0:T(1,128)} %bitcast.10, f32[32,128]{1,0:T(8,128)} %bitcast.9), custom_call_target="tpu_custom_call" | custom-call | tf_op jit(solution)/shard_map/pallas_call | solution.py:392
  86.5 0.0 copy-start
  86.5 2.4 %shard_map.78 = bf16[256,4096]{1,0:T(8,128)(2,1)} custom-call(bf16[256,4096]{1,0:T(8,128)(2,1)} %get-tuple-element.4.source), custom_call_target="tpu_custom_call" | custom-call | tf_op jit(solution)/shard_map/pallas_call | solution.py:433
  88.9 0.0 copy-done
  88.9 0.5 copy.10
Async XLA Ops:
  86.5 2.4 %copy-start = (f32[1,8]{1,0:T(1,128)S(1)}, f32[1,8]{1,0:T(1,128)}, u32[]{:S(2)}) copy-start(f32[1,8]{1,0:T(1,128)} %get-tuple-element.5) | copy-start | bytes 100
